TPU v7x, 32 devices: a whole 2x2x4 slice. The times are simulated.
32 devices in a mesh: groups: 2 (over x), ctx: 16 (over z, y, core).
Axes of the slice: x: 2, y: 2, z: 4, core: 2. Of those that a mesh axis runs over, the one named last changes fastest.
Arguments:
- queries: bfloat16 [16384, 2048], P(('groups', 'ctx')), parts along dimension 0, may hold values from -400 to 400
- keys: bfloat16 [16384, 512], P(('groups', 'ctx')), parts along dimension 0, may hold values from -8 to 8
- values: bfloat16 [16384, 512], P(('groups', 'ctx')), parts along dimension 0, may hold values from -6 to 6
- grad_out: bfloat16 [16384, 2048], P(('groups', 'ctx')), parts along dimension 0, may hold values from -6 to 6
- seg_starts: int32 [32], P('groups'), parts along dimension 0, may hold values from 0 to 8191, as said below
- channels: int32 [16384], P(('groups', 'ctx')), parts along dimension 0, may hold values from 0 to 1
Outputs:
- grad_queries: bfloat16 [16384, 2048], P(('groups', 'ctx')), parts along dimension 0
- grad_keys: bfloat16 [16384, 512], P(('groups', 'ctx')), parts along dimension 0
- grad_values: bfloat16 [16384, 512], P(('groups', 'ctx')), parts along dimension 0
There are 2 independent parts, one for each index of `groups`. A program takes and returns all parts, laid end to end along the dimension named above; each array names one. Nothing has to cross between parts.
Inputs may be any that keep to these rules, and one draw needn't show every extreme that they name: seg_starts[0] is 0 and the entries rise strictly; segment s runs from seg_starts[s] to the next start or the stream's end.
All inputs are finite; a program needn't handle non-finite values.
Results may differ from a plain program's by a relative error of at most 0.0055.
Values may be sent and summed in bfloat16 or wider, within the bound.
A program may use at most 128 MiB of HBM per device.

v0:
```python
import jax
import jax.numpy as jnp
from jax import lax
from jax.sharding import PartitionSpec as P

HQ = 16
HK = 4
HD = 128
LAG = 16


def shifted(value, axis, steps):
    count = lax.axis_size(axis)
    first, last = (max(0, -steps), min(count, count - steps))
    return lax.ppermute(value, axis, [(source, source + steps) for source in range(first, last)])


def score_block(query_group, key_group):
    head_scale = query_group.shape[-1] ** (-0.5)
    return (
        jnp.einsum("igd,jd->gij", query_group, key_group, preferred_element_type=jnp.float32)
        * head_scale
    )


def finish(query_group, grad_group, key_group, probs, dprobs, delta):
    head_scale = query_group.shape[-1] ** (-0.5)
    dscores = (probs * (dprobs - delta[..., None])).astype(jnp.bfloat16)
    probs_low = probs.astype(jnp.bfloat16)
    grad_query = (
        jnp.einsum("gij,jd->igd", dscores, key_group, preferred_element_type=jnp.float32)
        * head_scale
    )
    grad_key = (
        jnp.einsum("gij,igd->jd", dscores, query_group, preferred_element_type=jnp.float32)
        * head_scale
    )
    grad_value = jnp.einsum(
        "gij,igd->jd", probs_low, grad_group, preferred_element_type=jnp.float32
    )
    return (grad_query, grad_key, grad_value)


def statistics(query_group, grad_group, key_group, value_group, visible_mask):
    scores = score_block(query_group, key_group)
    row_max = jnp.max(jnp.where(visible_mask[None], scores, -1e30), axis=-1)
    weights = jnp.where(visible_mask[None], jnp.exp(scores - row_max[..., None]), 0.0)
    row_sum = jnp.sum(weights, axis=-1)
    safe_sum = jnp.where(row_sum > 0.0, row_sum, 1.0)
    probs = weights / safe_sum[..., None]
    dprobs = jnp.einsum("igd,jd->gij", grad_group, value_group, preferred_element_type=jnp.float32)
    delta = jnp.sum(probs * dprobs, axis=-1)
    return (probs, dprobs, row_max, safe_sum, delta)


def whole_window(query_group, grad_group, key_group, value_group, visible_mask):
    probs, dprobs, row_max, safe_sum, delta = statistics(
        query_group, grad_group, key_group, value_group, visible_mask
    )
    return finish(query_group, grad_group, key_group, probs, dprobs, delta)


def per_device(queries, keys, values, grad_out, seg_starts, channels):
    block_rows = queries.shape[0]
    group_size = HQ // HK
    device_index = lax.axis_index("ctx")
    stream_len = block_rows * lax.axis_size("ctx")
    first_row = device_index * block_rows
    offsets = jnp.arange(block_rows, dtype=jnp.int32)
    query_pos = first_row + offsets
    prev_pos = first_row - block_rows + offsets

    def segment_of(positions):
        return jnp.sum((seg_starts[None, :] <= positions[:, None]).astype(jnp.int32), axis=1) - 1

    def visible(later_pos, later_chan, earlier_pos, earlier_chan):
        later = later_pos[:, None]
        earlier = earlier_pos[None, :]
        allowed = (
            (earlier <= later)
            & (earlier > later - block_rows)
            & (earlier >= 0)
            & (later < stream_len)
        )
        allowed = allowed & (segment_of(later_pos)[:, None] == segment_of(earlier_pos)[None, :])
        return allowed & ((later_chan[:, None] == earlier_chan[None, :]) | (earlier <= later - LAG))

    def split_rows(matrix):
        return matrix.reshape(block_rows, HK, group_size, HD).transpose(1, 0, 2, 3)

    def split_keys(matrix):
        return matrix.reshape(matrix.shape[0], HK, HD).transpose(1, 0, 2)

    def join_keys(stacked):
        return stacked.transpose(1, 0, 2).reshape(block_rows, HK * HD)

    prev_keys, prev_values, prev_chan = shifted((keys, values, channels), "ctx", 1)
    query_heads = split_rows(queries)
    grad_heads = split_rows(grad_out)
    own_key_heads = split_keys(keys)
    own_value_heads = split_keys(values)
    prev_key_heads = split_keys(prev_keys)
    prev_value_heads = split_keys(prev_values)
    mask_prev = visible(query_pos, channels, prev_pos, prev_chan)
    mask_own = visible(query_pos, channels, query_pos, channels)
    window_mask = jnp.concatenate([mask_prev, mask_own], axis=1)
    key_window = jnp.concatenate([prev_key_heads, own_key_heads], axis=1)
    value_window = jnp.concatenate([prev_value_heads, own_value_heads], axis=1)

    def window_step(inputs):
        return whole_window(inputs[0], inputs[1], inputs[2], inputs[3], window_mask)

    grad_query, grad_key, grad_value = lax.map(
        window_step, (query_heads, grad_heads, key_window, value_window)
    )
    back_key, back_value = shifted(
        (grad_key[:, :block_rows], grad_value[:, :block_rows]), "ctx", -1
    )
    grad_key_own = grad_key[:, block_rows:]
    grad_value_own = grad_value[:, block_rows:]
    grad_keys = grad_key_own + back_key
    grad_values = grad_value_own + back_value
    return (
        grad_query.transpose(1, 0, 2, 3).reshape(block_rows, HQ * HD).astype(jnp.bfloat16),
        join_keys(grad_keys).astype(jnp.bfloat16),
        join_keys(grad_values).astype(jnp.bfloat16),
    )


def solution(mesh):
    placed = (
        P(("groups", "ctx"), None),
        P(("groups", "ctx"), None),
        P(("groups", "ctx"), None),
        P(("groups", "ctx"), None),
        P("groups"),
        P(("groups", "ctx")),
    )
    return jax.shard_map(
        per_device,
        mesh=mesh,
        in_specs=placed,
        out_specs=(
            P(("groups", "ctx"), None),
            P(("groups", "ctx"), None),
            P(("groups", "ctx"), None),
        ),
        check_vma=False,
    )
```

profile of v0, /device:TPU:13, one launch (start us, length us, event | category | flops | bytes accessed | tf_op | source)
XLA Modules:
  0.0 149.1 jit_solution(6259175591848619039)
XLA Ops:
  0.7 3.8 %collective-permute-start.1 = (s32[512]{0:T(512)}, s32[512]{0:T(512)S(1)}, u32[]{:S(2)}, u32[]{:S(2)}) collective-permute-start(s32[512]{0:T(512)} %param.13), channel_id=1, source_target_pairs={{0,1},{1,2},{2,3},{3,4},{4,5},{5,6},{6,7},{7,8},{8,9},{9,10},{10,1... | collective-permute-start | bytes 6152 | tf_op jit(solution)/shard_map/ppermute | solution.py:15
  9.8 3.5 %collective-permute-start.2 = (bf16[512,512]{0,1:T(8,128)(2,1)}, bf16[512,512]{0,1:T(8,128)(2,1)}, u32[]{:S(2)}, u32[]{:S(2)}) collective-permute-start(bf16[512,512]{0,1:T(8,128)(2,1)} %copy.34), channel_id=1, source_target_pairs={{0,1},{1,2},{2,3},{3,4},{4,5},{5,6},{6,7},{7,8},{8,9},{9,10},{10,1... | collective-permute-start | bytes 1572872 | tf_op jit(solution)/shard_map/ppermute | solution.py:15
  13.5 2.5 %copy.33 = bf16[512,2048]{0,1:T(8,128)(2,1)} copy(bf16[512,2048]{1,0:T(8,128)(2,1)S(1)} %copy-done) | data formatting | bytes 4194304 | tf_op args[0]
  16.0 3.9 %copy.36 = bf16[512,2048]{0,1:T(8,128)(2,1)} copy(bf16[512,2048]{1,0:T(8,128)(2,1)} %param.11) | data formatting | bytes 4194304 | tf_op args[3]
  26.9 90.4 %while.14 = (s32[]{:T(128)}, bf16[4,512,4,128]{1,3,2,0:T(8,128)(2,1)}, f32[4,1024,128]{2,1,0:T(8,128)}, f32[4,1024,128]{2,1,0:T(8,128)}, bf16[4,1024,128]{1,2,0:...) while((s32[]{:T(128)}, ...), condition=%wide.region_6.7_spmd, body=%wide.region_2.6_spmd.sunk | while | flops 3253079040 | bytes 111745232 | solution.py:113
  26.9 6.9 %fusion.111 = (f32[4,512]{1,0:T(4,128)S(1)}, f32[4,512,1024]{1,2,0:T(8,128)}) fusion(pred[512,1024]{0,1:T(8,128)(4,1)} %get-tuple-element.193, bf16[4,512,4,128]{1,3,2,0:T(8,128)(2,1)S(1)} %get-tuple-element.194, s32[]{:T(128)} %get-tuple-element.178, bf16[4,1024,128]{1,2,0:T(8,128)(2,1)S(1)} %get-tuple-element.192), kind=kOutput, calls=%fused_computation.79.clone.1 | convolution fusion | flops 1086325760 | bytes 11020288 | tf_op jit(solution)/shard_map/while/body/eval_jaxpr/sub | solution.py:47
  33.8 5.1 %fusion.112 = (f32[4,512]{1,0:T(4,128)S(1)}, f32[1024,512,4]{1,0,2:T(8,128)S(1)}) fusion(f32[4,512,1024]{1,2,0:T(8,128)} %get-tuple-element.164, f32[4,512]{1,0:T(4,128)S(1)} %compare_select_fusion.2, bf16[4,512,4,128]{1,3,2,0:T(8,128)(2,1)} %get-tuple-element.196, s32[]{:T(128)} %get-tuple-element.178, bf16[4,1024,128]{1,2,0:T(8,128)(2,1)} %get-tuple-element.195), kind=kOutput, calls=%fused_computation.3.clone.1 | convolution fusion | flops 543160320 | bytes 17581056 | tf_op jit(solution)/shard_map/while/body/eval_jaxpr/igd,jd->gij/dot_general | solution.py:51
  46.4 3.1 %fusion.116 = f32[4,1024,128]{2,1,0:T(8,128)} fusion(f32[4,1024,128]{2,1,0:T(8,128)} %get-tuple-element.181, s32[]{:T(128)} %get-tuple-element.178, bf16[4,512,4,128]{1,3,2,0:T(8,128)(2,1)} %get-tuple-element.196, f32[4,512,1024]{1,2,0:T(8,128)S(1)} %bitcast.169, f32[4,512]{1,0:T(4,128)S(1)} %compare_select_fusion.2), kind=kOutput, calls=%fused_computation.22.clone.1 | convolution fusion | flops 541065216 | bytes 9446400 | tf_op jit(solution)/shard_map/while/body/eval_jaxpr/gij,igd->jd/dot_general | solution.py:38
  49.5 6.9 %fusion.111 = (f32[4,512]{1,0:T(4,128)S(1)}, f32[4,512,1024]{1,2,0:T(8,128)}) fusion(pred[512,1024]{0,1:T(8,128)(4,1)} %get-tuple-element.193, bf16[4,512,4,128]{1,3,2,0:T(8,128)(2,1)S(1)} %get-tuple-element.194, s32[]{:T(128)} %get-tuple-element.178, bf16[4,1024,128]{1,2,0:T(8,128)(2,1)S(1)} %get-tuple-element.192), kind=kOutput, calls=%fused_computation.79.clone.1 | convolution fusion | flops 1086325760 | bytes 11020288 | tf_op jit(solution)/shard_map/while/body/eval_jaxpr/sub | solution.py:47
  56.4 5.1 %fusion.112 = (f32[4,512]{1,0:T(4,128)S(1)}, f32[1024,512,4]{1,0,2:T(8,128)S(1)}) fusion(f32[4,512,1024]{1,2,0:T(8,128)} %get-tuple-element.164, f32[4,512]{1,0:T(4,128)S(1)} %compare_select_fusion.2, bf16[4,512,4,128]{1,3,2,0:T(8,128)(2,1)} %get-tuple-element.196, s32[]{:T(128)} %get-tuple-element.178, bf16[4,1024,128]{1,2,0:T(8,128)(2,1)} %get-tuple-element.195), kind=kOutput, calls=%fused_computation.3.clone.1 | convolution fusion | flops 543160320 | bytes 17581056 | tf_op jit(solution)/shard_map/while/body/eval_jaxpr/igd,jd->gij/dot_general | solution.py:51
  62.5 2.4 %fusion.113 = bf16[4,512,1024]{1,2,0:T(8,128)(2,1)S(1)} fusion(f32[1024,512,4]{1,0,2:T(8,128)S(1)} %get-tuple-element.166, f32[4,512]{1,0:T(4,128)S(1)} %get-tuple-element.167, f32[4,512,1024]{1,2,0:T(8,128)S(1)} %bitcast.169, f32[4,512]{1,0:T(4,128)S(1)} %compare_select_fusion.2), kind=kLoop, calls=%fused_computation.5.clone.1 | loop fusion | flops 8388608 | bytes 20987904 | tf_op jit(solution)/shard_map/while/body/eval_jaxpr/convert_element_type | solution.py:28
  69.0 3.1 %fusion.116 = f32[4,1024,128]{2,1,0:T(8,128)} fusion(f32[4,1024,128]{2,1,0:T(8,128)} %get-tuple-element.181, s32[]{:T(128)} %get-tuple-element.178, bf16[4,512,4,128]{1,3,2,0:T(8,128)(2,1)} %get-tuple-element.196, f32[4,512,1024]{1,2,0:T(8,128)S(1)} %bitcast.169, f32[4,512]{1,0:T(4,128)S(1)} %compare_select_fusion.2), kind=kOutput, calls=%fused_computation.22.clone.1 | convolution fusion | flops 541065216 | bytes 9446400 | tf_op jit(solution)/shard_map/while/body/eval_jaxpr/gij,igd->jd/dot_general | solution.py:38
  72.1 6.9 %fusion.111 = (f32[4,512]{1,0:T(4,128)S(1)}, f32[4,512,1024]{1,2,0:T(8,128)}) fusion(pred[512,1024]{0,1:T(8,128)(4,1)} %get-tuple-element.193, bf16[4,512,4,128]{1,3,2,0:T(8,128)(2,1)S(1)} %get-tuple-element.194, s32[]{:T(128)} %get-tuple-element.178, bf16[4,1024,128]{1,2,0:T(8,128)(2,1)S(1)} %get-tuple-element.192), kind=kOutput, calls=%fused_computation.79.clone.1 | convolution fusion | flops 1086325760 | bytes 11020288 | tf_op jit(solution)/shard_map/while/body/eval_jaxpr/sub | solution.py:47
  79.0 5.1 %fusion.112 = (f32[4,512]{1,0:T(4,128)S(1)}, f32[1024,512,4]{1,0,2:T(8,128)S(1)}) fusion(f32[4,512,1024]{1,2,0:T(8,128)} %get-tuple-element.164, f32[4,512]{1,0:T(4,128)S(1)} %compare_select_fusion.2, bf16[4,512,4,128]{1,3,2,0:T(8,128)(2,1)} %get-tuple-element.196, s32[]{:T(128)} %get-tuple-element.178, bf16[4,1024,128]{1,2,0:T(8,128)(2,1)} %get-tuple-element.195), kind=kOutput, calls=%fused_computation.3.clone.1 | convolution fusion | flops 543160320 | bytes 17581056 | tf_op jit(solution)/shard_map/while/body/eval_jaxpr/igd,jd->gij/dot_general | solution.py:51
  91.6 3.1 %fusion.116 = f32[4,1024,128]{2,1,0:T(8,128)} fusion(f32[4,1024,128]{2,1,0:T(8,128)} %get-tuple-element.181, s32[]{:T(128)} %get-tuple-element.178, bf16[4,512,4,128]{1,3,2,0:T(8,128)(2,1)} %get-tuple-element.196, f32[4,512,1024]{1,2,0:T(8,128)S(1)} %bitcast.169, f32[4,512]{1,0:T(4,128)S(1)} %compare_select_fusion.2), kind=kOutput, calls=%fused_computation.22.clone.1 | convolution fusion | flops 541065216 | bytes 9446400 | tf_op jit(solution)/shard_map/while/body/eval_jaxpr/gij,igd->jd/dot_general | solution.py:38
  94.7 6.9 %fusion.111 = (f32[4,512]{1,0:T(4,128)S(1)}, f32[4,512,1024]{1,2,0:T(8,128)}) fusion(pred[512,1024]{0,1:T(8,128)(4,1)} %get-tuple-element.193, bf16[4,512,4,128]{1,3,2,0:T(8,128)(2,1)S(1)} %get-tuple-element.194, s32[]{:T(128)} %get-tuple-element.178, bf16[4,1024,128]{1,2,0:T(8,128)(2,1)S(1)} %get-tuple-element.192), kind=kOutput, calls=%fused_computation.79.clone.1 | convolution fusion | flops 1086325760 | bytes 11020288 | tf_op jit(solution)/shard_map/while/body/eval_jaxpr/sub | solution.py:47
  101.6 5.1 %fusion.112 = (f32[4,512]{1,0:T(4,128)S(1)}, f32[1024,512,4]{1,0,2:T(8,128)S(1)}) fusion(f32[4,512,1024]{1,2,0:T(8,128)} %get-tuple-element.164, f32[4,512]{1,0:T(4,128)S(1)} %compare_select_fusion.2, bf16[4,512,4,128]{1,3,2,0:T(8,128)(2,1)} %get-tuple-element.196, s32[]{:T(128)} %get-tuple-element.178, bf16[4,1024,128]{1,2,0:T(8,128)(2,1)} %get-tuple-element.195), kind=kOutput, calls=%fused_computation.3.clone.1 | convolution fusion | flops 543160320 | bytes 17581056 | tf_op jit(solution)/shard_map/while/body/eval_jaxpr/igd,jd->gij/dot_general | solution.py:51
  114.2 3.1 %fusion.116 = f32[4,1024,128]{2,1,0:T(8,128)} fusion(f32[4,1024,128]{2,1,0:T(8,128)} %get-tuple-element.181, s32[]{:T(128)} %get-tuple-element.178, bf16[4,512,4,128]{1,3,2,0:T(8,128)(2,1)} %get-tuple-element.196, f32[4,512,1024]{1,2,0:T(8,128)S(1)} %bitcast.169, f32[4,512]{1,0:T(4,128)S(1)} %compare_select_fusion.2), kind=kOutput, calls=%fused_computation.22.clone.1 | convolution fusion | flops 541065216 | bytes 9446400 | tf_op jit(solution)/shard_map/while/body/eval_jaxpr/gij,igd->jd/dot_general | solution.py:38
  117.3 2.4 %slice.15 = f32[4,512,128]{2,1,0:T(8,128)} slice(f32[4,1024,128]{2,1,0:T(8,128)} %get-tuple-element.54), slice={[0:4], [0:512], [0:128]} | slice | bytes 2097152 | tf_op jit(solution)/shard_map/slice | solution.py:117
  122.7 2.5 %collective-permute-start.3 = (f32[4,512,128]{2,1,0:T(8,128)}, f32[4,512,128]{2,1,0:T(8,128)S(1)}, u32[]{:S(2)}, u32[]{:S(2)}) collective-permute-start(f32[4,512,128]{2,1,0:T(8,128)} %slice.13), channel_id=1, source_target_pairs={{1,0},{2,1},{3,2},{4,3},{5,4},{6,5},{7,6},{8,7},{9,8},{10,9},{11,1... | collective-permute-start | bytes 3145736 | tf_op jit(solution)/shard_map/ppermute | solution.py:15
  125.2 2.4 %copy.47 = bf16[512,2048]{1,0:T(8,128)(2,1)} copy(bf16[512,2048]{0,1:T(8,128)(2,1)S(1)} %bitcast.172) | data formatting | bytes 4194304 | tf_op jit(solution)/shard_map/convert_element_type | solution.py:124
  127.6 9.5 %collective-permute-done.4 = f32[4,512,128]{2,1,0:T(8,128)} collective-permute-done((f32[4,512,128]{2,1,0:T(8,128)}, f32[4,512,128]{2,1,0:T(8,128)}, u32[]{:S(2)}, u32[]{:S(2)}) %collective-permute-start.4) | collective-permute-done | bytes 1048608 | tf_op jit(solution)/shard_map/ppermute | solution.py:15
  137.0 2.4 %copy_bitcast_fusion = bf16[512,512]{1,0:T(8,128)(2,1)} fusion(f32[4,512,128]{2,1,0:T(8,128)} %collective-permute-done.4, f32[4,1024,128]{2,1,0:T(8,128)} %get-tuple-element.54), kind=kLoop, calls=%fused_computation.66 | loop fusion | flops 524288 | bytes 2621440 | tf_op jit(solution)/shard_map/convert_element_type | solution.py:126
  139.5 8.7 %collective-permute-done.3 = f32[4,512,128]{2,1,0:T(8,128)S(1)} collective-permute-done((f32[4,512,128]{2,1,0:T(8,128)}, f32[4,512,128]{2,1,0:T(8,128)S(1)}, u32[]{:S(2)}, u32[]{:S(2)}) %collective-permute-start.3) | collective-permute-done | bytes 1048608 | tf_op jit(solution)/shard_map/ppermute | solution.py:15
  (92 shorter events, 43.7 us)
Async XLA Ops:
  0.6 12.7 %copy-start.10 = (s32[16]{0:T(128)S(1)}, s32[16]{0:T(128)}, u32[]{:S(2)}) copy-start(s32[16]{0:T(128)} %param.12) | copy-start | bytes 196
  0.6 12.9 %copy-start = (bf16[512,2048]{1,0:T(8,128)(2,1)S(1)}, bf16[512,2048]{1,0:T(8,128)(2,1)}, u32[]{:S(2)}) copy-start(bf16[512,2048]{1,0:T(8,128)(2,1)} %param.8) | copy-start | bytes 6291460
  0.7 19.3 %collective-permute-start.1 = (s32[512]{0:T(512)}, s32[512]{0:T(512)S(1)}, u32[]{:S(2)}, u32[]{:S(2)}) collective-permute-start(s32[512]{0:T(512)} %param.13), channel_id=1, source_target_pairs={{0,1},{1,2},{2,3},{3,4},{4,5},{5,6},{6,7},{7,8},{8,9},{9,10},{10,1... | collective-permute-start | bytes 6152 | tf_op jit(solution)/shard_map/ppermute | solution.py:15
  5.8 10.3 %copy-start.7 = (bf16[512,512]{0,1:T(8,128)(2,1)}, bf16[512,512]{0,1:T(8,128)(2,1)S(1)}, u32[]{:S(2)}) copy-start(bf16[512,512]{0,1:T(8,128)(2,1)S(1)} %copy.31) | copy-start | bytes 1572868
  5.8 16.5 %collective-permute-start = (bf16[512,512]{0,1:T(8,128)(2,1)S(1)}, bf16[512,512]{0,1:T(8,128)(2,1)S(1)}, u32[]{:S(2)}, u32[]{:S(2)}) collective-permute-start(bf16[512,512]{0,1:T(8,128)(2,1)S(1)} %copy.31), channel_id=1, source_target_pairs={{0,1},{1,2},{2,3},{3,4},{4,5},{5,6},{6,7},{7,8},{8,9},{9,10},{10,1... | collective-permute-start | bytes 1572872 | tf_op jit(solution)/shard_map/ppermute | solution.py:15
  9.8 14.8 %collective-permute-start.2 = (bf16[512,512]{0,1:T(8,128)(2,1)}, bf16[512,512]{0,1:T(8,128)(2,1)}, u32[]{:S(2)}, u32[]{:S(2)}) collective-permute-start(bf16[512,512]{0,1:T(8,128)(2,1)} %copy.34), channel_id=1, source_target_pairs={{0,1},{1,2},{2,3},{3,4},{4,5},{5,6},{6,7},{7,8},{8,9},{9,10},{10,1... | collective-permute-start | bytes 1572872 | tf_op jit(solution)/shard_map/ppermute | solution.py:15
  16.0 3.9 %copy-start.9 = (s32[512]{0:T(512)S(1)}, s32[512]{0:T(512)}, u32[]{:S(2)}) copy-start(s32[512]{0:T(512)} %param.13) | copy-start | bytes 6148
  23.1 3.8 %copy-start.1 = (bf16[512,2048]{0,1:T(8,128)(2,1)S(1)}, bf16[512,2048]{0,1:T(8,128)(2,1)}, u32[]{:S(2)}) copy-start(bf16[512,2048]{0,1:T(8,128)(2,1)} %copy.33) | copy-start | bytes 6291460
  33.8 5.1 %slice-start = ((s8[8388608]{0:T(1024)(128)(4,1)}), s8[4194304]{0:T(1024)(128)(4,1)S(1)}, s32[]{:S(2)}) async-start(s8[8388608]{0:T(1024)(128)(4,1)} %bitcast.168), calls=%async_computation | async-start | bytes 8388608 | tf_op jit(solution)/shard_map/while
  33.8 6.1 %slice-start.1 = ((s8[8388608]{0:T(1024)(128)(4,1)}), s8[4194304]{0:T(1024)(128)(4,1)S(1)}, s32[]{:S(2)}) async-start(s8[8388608]{0:T(1024)(128)(4,1)} %bitcast.168), calls=%async_computation.1 | async-start | bytes 8388608 | tf_op jit(solution)/shard_map/while
  42.3 2.1 %copy-start.2 = (bf16[4,512,4,128]{1,3,2,0:T(8,128)(2,1)S(1)}, bf16[4,512,4,128]{1,3,2,0:T(8,128)(2,1)}, u32[]{:S(2)}) copy-start(bf16[4,512,4,128]{1,3,2,0:T(8,128)(2,1)} %get-tuple-element.179) | copy-start | bytes 6291460 | tf_op jit(solution)/shard_map/while
  56.4 5.1 %slice-start = ((s8[8388608]{0:T(1024)(128)(4,1)}), s8[4194304]{0:T(1024)(128)(4,1)S(1)}, s32[]{:S(2)}) async-start(s8[8388608]{0:T(1024)(128)(4,1)} %bitcast.168), calls=%async_computation | async-start | bytes 8388608 | tf_op jit(solution)/shard_map/while
  56.4 6.1 %slice-start.1 = ((s8[8388608]{0:T(1024)(128)(4,1)}), s8[4194304]{0:T(1024)(128)(4,1)S(1)}, s32[]{:S(2)}) async-start(s8[8388608]{0:T(1024)(128)(4,1)} %bitcast.168), calls=%async_computation.1 | async-start | bytes 8388608 | tf_op jit(solution)/shard_map/while
  79.0 5.1 %slice-start = ((s8[8388608]{0:T(1024)(128)(4,1)}), s8[4194304]{0:T(1024)(128)(4,1)S(1)}, s32[]{:S(2)}) async-start(s8[8388608]{0:T(1024)(128)(4,1)} %bitcast.168), calls=%async_computation | async-start | bytes 8388608 | tf_op jit(solution)/shard_map/while
  79.0 6.1 %slice-start.1 = ((s8[8388608]{0:T(1024)(128)(4,1)}), s8[4194304]{0:T(1024)(128)(4,1)S(1)}, s32[]{:S(2)}) async-start(s8[8388608]{0:T(1024)(128)(4,1)} %bitcast.168), calls=%async_computation.1 | async-start | bytes 8388608 | tf_op jit(solution)/shard_map/while
  87.5 2.1 %copy-start.2 = (bf16[4,512,4,128]{1,3,2,0:T(8,128)(2,1)S(1)}, bf16[4,512,4,128]{1,3,2,0:T(8,128)(2,1)}, u32[]{:S(2)}) copy-start(bf16[4,512,4,128]{1,3,2,0:T(8,128)(2,1)} %get-tuple-element.179) | copy-start | bytes 6291460 | tf_op jit(solution)/shard_map/while
  101.6 5.1 %slice-start = ((s8[8388608]{0:T(1024)(128)(4,1)}), s8[4194304]{0:T(1024)(128)(4,1)S(1)}, s32[]{:S(2)}) async-start(s8[8388608]{0:T(1024)(128)(4,1)} %bitcast.168), calls=%async_computation | async-start | bytes 8388608 | tf_op jit(solution)/shard_map/while
  101.6 6.1 %slice-start.1 = ((s8[8388608]{0:T(1024)(128)(4,1)}), s8[4194304]{0:T(1024)(128)(4,1)S(1)}, s32[]{:S(2)}) async-start(s8[8388608]{0:T(1024)(128)(4,1)} %bitcast.168), calls=%async_computation.1 | async-start | bytes 8388608 | tf_op jit(solution)/shard_map/while
  110.1 2.1 %copy-start.2 = (bf16[4,512,4,128]{1,3,2,0:T(8,128)(2,1)S(1)}, bf16[4,512,4,128]{1,3,2,0:T(8,128)(2,1)}, u32[]{:S(2)}) copy-start(bf16[4,512,4,128]{1,3,2,0:T(8,128)(2,1)} %get-tuple-element.179) | copy-start | bytes 6291460 | tf_op jit(solution)/shard_map/while
  117.3 4.3 %copy-start.5 = (f32[4,1024,128]{2,1,0:T(8,128)S(1)}, f32[4,1024,128]{2,1,0:T(8,128)}, u32[]{:S(2)}) copy-start(f32[4,1024,128]{2,1,0:T(8,128)} %get-tuple-element.53) | copy-start | bytes 6291460
  117.3 7.9 %copy-start.4 = (bf16[4,512,4,128]{1,3,2,0:T(8,128)(2,1)S(1)}, bf16[4,512,4,128]{1,3,2,0:T(8,128)(2,1)}, u32[]{:S(2)}) copy-start(bf16[4,512,4,128]{1,3,2,0:T(8,128)(2,1)} %get-tuple-element.52) | copy-start | bytes 6291460
  119.7 17.3 %collective-permute-start.4 = (f32[4,512,128]{2,1,0:T(8,128)}, f32[4,512,128]{2,1,0:T(8,128)}, u32[]{:S(2)}, u32[]{:S(2)}) collective-permute-start(f32[4,512,128]{2,1,0:T(8,128)} %slice.15), channel_id=1, source_target_pairs={{1,0},{2,1},{3,2},{4,3},{5,4},{6,5},{7,6},{8,7},{9,8},{10,9},{11,1... | collective-permute-start | bytes 3145736 | tf_op jit(solution)/shard_map/ppermute | solution.py:15
  122.7 25.5 %collective-permute-start.3 = (f32[4,512,128]{2,1,0:T(8,128)}, f32[4,512,128]{2,1,0:T(8,128)S(1)}, u32[]{:S(2)}, u32[]{:S(2)}) collective-permute-start(f32[4,512,128]{2,1,0:T(8,128)} %slice.13), channel_id=1, source_target_pairs={{1,0},{2,1},{3,2},{4,3},{5,4},{6,5},{7,6},{8,7},{9,8},{10,9},{11,1... | collective-permute-start | bytes 3145736 | tf_op jit(solution)/shard_map/ppermute | solution.py:15
  127.6 20.6 %copy-start.6 = (f32[4,1024,128]{2,1,0:T(8,128)S(1)}, f32[4,1024,128]{2,1,0:T(8,128)}, u32[]{:S(2)}) copy-start(f32[4,1024,128]{2,1,0:T(8,128)} %get-tuple-element.53) | copy-start | bytes 6291460
  (6 other events, 8.1 us)
where the time goes:
time: 150 us; the launch traced here: 149 us
  matrix products  71.4 us (48%)
  local copies, waits for them, and re-layouts  25.7 us (17%)
  other arithmetic  19 us (13%)
  waiting for transfers between devices  18.2 us (12%)
  starting transfers between devices  13.7 us (9%)
    sub x4, matrix products, statistics(): scores - row_max[..., None]  27.6 us
    dot_general x4, matrix products, statistics(): jnp.einsum('igd,jd->gij', grad_group, value_group, preferred_element_type...  20.3 us
    ppermute x5, waiting for transfers between devices, shifted(): lax.ppermute(value, axis, [(source, source + steps) for source in range(f...  18.2 us
    ppermute x5, starting transfers between devices, shifted(): lax.ppermute(value, axis, [(source, source + steps) for source in range(f...  13.7 us
    dot_general x4, matrix products, finish(): jnp.einsum('gij,igd->jd', probs_low, grad_group, preferred_element_type=j...  12.4 us
    unnamed x22, local copies, waits for them, and re-layouts  10.6 us
    convert_element_type x4, other arithmetic, finish(): dscores = (probs * (dprobs - delta[..., None])).astype(jnp.bfloat16)  9.5 us
    while x32, local copies, waits for them, and re-layouts  9.29 us
  transfers between devices with their start and end apart: 5, of which 2 were waited for; matrix products, arithmetic and copies ran while one was open for 13% of the time, Pallas kernels for 0%

commit v1 on v0

v1 whole, which is shorter than its diff:
```python
import functools

import jax
import jax.numpy as jnp
import numpy as np
from jax import lax
from jax.experimental import pallas as pl
from jax.experimental.pallas import tpu as pltpu
from jax.sharding import PartitionSpec as P

HQ = 16
HK = 4
HD = 128
LAG = 16
GROUP = HQ // HK
BLK = 128
MASKED = -1e30
SCALE = HD ** (-0.5)
EXP2_SCALE = float(SCALE * np.log2(np.e))

TRANS_B = (((1,), (1,)), ((), ()))
TRANS_A = (((0,), (0,)), ((), ()))


def kernel(
    count,
    seg_ref,
    chan_ref,
    q_hbm,
    k_hbm,
    v_hbm,
    g_hbm,
    gq_ref,
    gk_ref,
    gv_ref,
    q_ref,
    g_ref,
    kw_ref,
    vw_ref,
    chan_prev,
    bias_ref,
    dk_ref,
    dv_ref,
    back_send,
    back_recv,
    local_sem,
    fwd_send_sem,
    fwd_recv_sem,
    chan_sem,
    back_send_sem,
    back_recv_sem,
):
    rows = q_ref.shape[0]
    blocks = rows // BLK
    span = rows + BLK
    me = lax.axis_index("ctx")
    has_prev = me > 0
    has_next = me < count - 1

    def lanes(h, width):
        return pl.ds(pl.multiple_of(h * width, width), width)

    def local_copies(h):
        own = pl.ds(rows, rows)
        return (
            pltpu.make_async_copy(
                k_hbm.at[:, lanes(h, HD)], kw_ref.at[own, lanes(h, HD)], local_sem.at[0, h]
            ),
            pltpu.make_async_copy(
                v_hbm.at[:, lanes(h, HD)], vw_ref.at[own, lanes(h, HD)], local_sem.at[1, h]
            ),
            pltpu.make_async_copy(
                q_hbm.at[:, lanes(h, GROUP * HD)], q_ref.at[:, lanes(h, GROUP * HD)], local_sem.at[2, h]
            ),
            pltpu.make_async_copy(
                g_hbm.at[:, lanes(h, GROUP * HD)], g_ref.at[:, lanes(h, GROUP * HD)], local_sem.at[3, h]
            ),
        )

    def forward_copies(h):
        before = pl.ds(0, rows)
        return tuple(
            pltpu.make_async_remote_copy(
                src_ref=source.at[:, lanes(h, HD)],
                dst_ref=window.at[before, lanes(h, HD)],
                send_sem=fwd_send_sem.at[which, h],
                recv_sem=fwd_recv_sem.at[which, h],
                device_id={"ctx": me + 1},
                device_id_type=pl.DeviceIdType.MESH,
            )
            for which, (source, window) in enumerate(((k_hbm, kw_ref), (v_hbm, vw_ref)))
        )

    chan_copy = pltpu.make_async_remote_copy(
        src_ref=chan_ref,
        dst_ref=chan_prev,
        send_sem=chan_sem.at[0],
        recv_sem=chan_sem.at[1],
        device_id={"ctx": me + 1},
        device_id_type=pl.DeviceIdType.MESH,
    )

    def back_copy(h):
        return pltpu.make_async_remote_copy(
            src_ref=back_send.at[h],
            dst_ref=back_recv.at[h],
            send_sem=back_send_sem.at[h],
            recv_sem=back_recv_sem.at[h],
            device_id={"ctx": me - 1},
            device_id_type=pl.DeviceIdType.MESH,
        )

    barrier = pltpu.get_barrier_semaphore()

    @pl.when(has_prev)
    def _():
        pl.semaphore_signal(
            barrier, inc=1, device_id={"ctx": me - 1}, device_id_type=pl.DeviceIdType.MESH
        )

    @pl.when(has_next)
    def _():
        pl.semaphore_signal(
            barrier, inc=1, device_id={"ctx": me + 1}, device_id_type=pl.DeviceIdType.MESH
        )

    for h in range(HK):
        for copy in local_copies(h):
            copy.start()
    pl.semaphore_wait(barrier, has_prev.astype(jnp.int32) + has_next.astype(jnp.int32))

    @pl.when(has_next)
    def _():
        chan_copy.start()
        for h in range(HK):
            for copy in forward_copies(h):
                copy.start()

    @pl.when(jnp.logical_not(has_prev))
    def _():
        kw_ref[0:rows, :] = jnp.zeros((rows, HK * HD), jnp.bfloat16)
        vw_ref[0:rows, :] = jnp.zeros((rows, HK * HD), jnp.bfloat16)
        chan_prev[...] = jnp.zeros_like(chan_prev)

    @pl.when(has_prev)
    def _():
        chan_copy.wait_recv()

    def column(row):
        return jnp.transpose(jnp.broadcast_to(row, (BLK, BLK)))

    first_row = me * rows
    for b in range(blocks):
        here = slice(b * BLK, (b + 1) * BLK)
        position = first_row + b * BLK + lax.broadcasted_iota(jnp.int32, (1, BLK), 1)
        start = jnp.zeros((1, BLK), jnp.int32)
        for s in range(seg_ref.shape[0]):
            start = jnp.maximum(start, jnp.where(seg_ref[s] <= position, seg_ref[s], 0))
        start = start - (first_row - rows + b * BLK)
        query_chan = chan_ref[:, here]
        query = lax.broadcasted_iota(jnp.int32, (BLK, BLK), 1)
        for c in range(span // BLK):
            key = c * BLK + lax.broadcasted_iota(jnp.int32, (BLK, BLK), 0)
            place = (b + c) * BLK
            if place < rows:
                key_chan = chan_prev[:, place : place + BLK]
            else:
                key_chan = chan_ref[:, place - rows : place - rows + BLK]
            allowed = (key > query) & (key <= query + rows) & (key >= start)
            allowed = allowed & (
                (column(key_chan) == query_chan) | (key <= query + (rows - LAG))
            )
            bias_ref[b, c * BLK : (c + 1) * BLK, :] = jnp.where(allowed, 0.0, MASKED)

    def head_step(h, carry):
        for copy in local_copies(h):
            copy.wait()

        @pl.when(has_prev)
        def _():
            for copy in forward_copies(h):
                copy.wait_recv()

        for b in range(blocks):
            here = slice(b * BLK, (b + 1) * BLK)
            window = slice(b * BLK, b * BLK + span)
            key = kw_ref[window, lanes(h, HD)]
            value = vw_ref[window, lanes(h, HD)]
            bias = bias_ref[b]
            bias = jnp.concatenate([bias, bias], axis=1)
            grad_key = None
            grad_value = None
            for pair in range(GROUP // 2):
                heads = [h * GROUP + 2 * pair, h * GROUP + 2 * pair + 1]
                query = jnp.concatenate([q_ref[here, lanes(i, HD)] for i in heads], axis=0)
                grad = jnp.concatenate([g_ref[here, lanes(i, HD)] for i in heads], axis=0)
                scores = (
                    lax.dot_general(key, query, TRANS_B, preferred_element_type=jnp.float32) + bias
                )
                top = jnp.max(scores, axis=0, keepdims=True)
                weights = jnp.exp2((scores - top) * EXP2_SCALE)
                probs = weights * (1.0 / jnp.sum(weights, axis=0, keepdims=True))
                dprobs = lax.dot_general(value, grad, TRANS_B, preferred_element_type=jnp.float32)
                delta = jnp.sum(probs * dprobs, axis=0, keepdims=True)
                dscores = (probs * (dprobs - delta)).astype(jnp.bfloat16)
                probs_low = probs.astype(jnp.bfloat16)
                grad_query = lax.dot_general(
                    dscores, key, TRANS_A, preferred_element_type=jnp.float32
                )
                grad_query = (grad_query * SCALE).astype(jnp.bfloat16)
                for k, i in enumerate(heads):
                    gq_ref[here, lanes(i, HD)] = grad_query[k * BLK : (k + 1) * BLK]
                key_term = jnp.dot(dscores, query, preferred_element_type=jnp.float32)
                value_term = jnp.dot(probs_low, grad, preferred_element_type=jnp.float32)
                grad_key = key_term if grad_key is None else grad_key + key_term
                grad_value = value_term if grad_value is None else grad_value + value_term
            shared = slice(b * BLK, b * BLK + rows)
            fresh = slice(b * BLK + rows, b * BLK + span)
            for total, term in ((dk_ref, grad_key), (dv_ref, grad_value)):
                if b == 0:
                    total[h, shared, :] = term[:rows]
                else:
                    total[h, shared, :] += term[:rows]
                total[h, fresh, :] = term[rows:]

        back_send[h, 0] = (dk_ref[h, 0:rows, :] * SCALE).astype(jnp.bfloat16)
        back_send[h, 1] = dv_ref[h, 0:rows, :].astype(jnp.bfloat16)

        @pl.when(has_prev)
        def _():
            back_copy(h).start()

        return carry

    lax.fori_loop(0, HK, head_step, 0)

    @pl.when(jnp.logical_not(has_next))
    def _():
        back_recv[...] = jnp.zeros_like(back_recv)

    for h in range(HK):

        @pl.when(has_next)
        def _():
            back_copy(h).wait_recv()

        columns = slice(h * HD, (h + 1) * HD)
        gk_ref[:, columns] = (
            dk_ref[h, rows:, :] * SCALE + back_recv[h, 0].astype(jnp.float32)
        ).astype(jnp.bfloat16)
        gv_ref[:, columns] = (
            dv_ref[h, rows:, :] + back_recv[h, 1].astype(jnp.float32)
        ).astype(jnp.bfloat16)

    @pl.when(has_next)
    def _():
        chan_copy.wait_send()
        for h in range(HK):
            for copy in forward_copies(h):
                copy.wait_send()

    @pl.when(has_prev)
    def _():
        for h in range(HK):
            back_copy(h).wait_send()


def per_device(queries, keys, values, grad_out, seg_starts, channels):
    rows = queries.shape[0]
    blocks = rows // BLK
    span = rows + BLK
    vmem = pl.BlockSpec(memory_space=pltpu.VMEM)
    hbm = pl.BlockSpec(memory_space=pl.ANY)
    return pl.pallas_call(
        functools.partial(kernel, lax.axis_size("ctx")),
        out_shape=(
            jax.ShapeDtypeStruct(queries.shape, jnp.bfloat16),
            jax.ShapeDtypeStruct(keys.shape, jnp.bfloat16),
            jax.ShapeDtypeStruct(values.shape, jnp.bfloat16),
        ),
        in_specs=[pl.BlockSpec(memory_space=pltpu.SMEM), vmem, hbm, hbm, hbm, hbm],
        out_specs=(vmem, vmem, vmem),
        scratch_shapes=[
            pltpu.VMEM((rows, HQ * HD), jnp.bfloat16),
            pltpu.VMEM((rows, HQ * HD), jnp.bfloat16),
            pltpu.VMEM((2 * rows, HK * HD), jnp.bfloat16),
            pltpu.VMEM((2 * rows, HK * HD), jnp.bfloat16),
            pltpu.VMEM((1, rows), jnp.int32),
            pltpu.VMEM((blocks, span, BLK), jnp.float32),
            pltpu.VMEM((HK, 2 * rows, HD), jnp.float32),
            pltpu.VMEM((HK, 2 * rows, HD), jnp.float32),
            pltpu.VMEM((HK, 2, rows, HD), jnp.bfloat16),
            pltpu.VMEM((HK, 2, rows, HD), jnp.bfloat16),
            pltpu.SemaphoreType.DMA((4, HK)),
            pltpu.SemaphoreType.DMA((2, HK)),
            pltpu.SemaphoreType.DMA((2, HK)),
            pltpu.SemaphoreType.DMA((2,)),
            pltpu.SemaphoreType.DMA((HK,)),
            pltpu.SemaphoreType.DMA((HK,)),
        ],
        compiler_params=pltpu.CompilerParams(
            collective_id=0, has_side_effects=True, vmem_limit_bytes=56 * 1024 * 1024
        ),
        name="window_backward",
    )(seg_starts, channels.reshape(1, rows), queries, keys, values, grad_out)


def solution(mesh):
    placed = (
        P(("groups", "ctx"), None),
        P(("groups", "ctx"), None),
        P(("groups", "ctx"), None),
        P(("groups", "ctx"), None),
        P("groups"),
        P(("groups", "ctx")),
    )
    return jax.shard_map(
        per_device,
        mesh=mesh,
        in_specs=placed,
        out_specs=(
            P(("groups", "ctx"), None),
            P(("groups", "ctx"), None),
            P(("groups", "ctx"), None),
        ),
        check_vma=False,
    )
```

time: 150 us -> 48.2 us (0.32)
  matrix products: 71.4 us -> 0 us
  Pallas kernels: 0 us -> 42.5 us
  local copies, waits for them, and re-layouts: 25.7 us -> 4.84 us
  other arithmetic: 19 us -> 0 us
  waiting for transfers between devices: 18.2 us -> 0 us
  starting transfers between devices: 13.7 us -> 0 us
    dot_general x16 -> x0, matrix products: 43.8 us -> none  [the longest x4 20.3 us: statistics(): jnp.einsum('igd,jd->gij', grad_group, value_group, preferred_element_type...]
    pallas_call x0 -> x1, Pallas kernels: none -> 42.5 us  [per_device(): pl.pallas_call(functools.partial(kernel, lax.axis_size('ctx')), out_shape...]
    sub x4 -> x0, matrix products: 27.6 us -> none  [statistics(): scores - row_max[..., None]]
    ppermute x5 -> x0, waiting for transfers between devices: 18.2 us -> none  [shifted(): lax.ppermute(value, axis, [(source, source + steps) for source in range(f...]
    ppermute x5 -> x0, starting transfers between devices: 13.7 us -> none  [shifted(): lax.ppermute(value, axis, [(source, source + steps) for source in range(f...]
    convert_element_type x6 -> x0, other arithmetic: 12.8 us -> none  [the longest x4 9.5 us: finish(): dscores = (probs * (dprobs - delta[..., None])).astype(jnp.bfloat16)]
    while x32 -> x0, local copies, waits for them, and re-layouts: 9.29 us -> none
    unnamed x22 -> x7, local copies, waits for them, and re-layouts: 10.6 us -> 4.84 us
  transfers between devices with their start and end apart: 5 -> 0, of which waited for: 2 -> 0; matrix products, arithmetic and copies ran while one was open for 13% -> 0% of each run, Pallas kernels for 0% -> 0%
where the time goes in v1:
time: 48.2 us; the launch traced here: 48 us
  Pallas kernels  42.5 us (88%)
  local copies, waits for them, and re-layouts  4.84 us (10%)
  between operations  0.66 us (1%)
    pallas_call x1, Pallas kernels, per_device(): pl.pallas_call(functools.partial(kernel, lax.axis_size('ctx')), out_shape...  42.5 us
    unnamed x7, local copies, waits for them, and re-layouts  4.84 us

profile of v1, /device:TPU:13, one launch (start us, length us, event | category | flops | bytes accessed | tf_op | source)
XLA Modules:
  0.0 48.0 jit_solution(6113456352554501942)
XLA Ops:
  0.6 42.5 %window_backward.1 = (bf16[512,2048]{1,0:T(8,128)(2,1)}, bf16[512,512]{1,0:T(8,128)(2,1)}, bf16[512,512]{1,0:T(8,128)(2,1)}) custom-call(s32[16]{0:T(128)} %seg_ref.1, s32[1,512]{1,0:T(1,128)} %bitcast.1, bf16[512,2048]{1,0:T(8,128)(2,1)} %q_hbm.1, bf16[512,512]{1,0:T(8,128)(2,1)} %k_hbm.1, bf16[512,512]{1,0:T(8,128)(2,1)} %v_hbm.1, bf16[512,2048]{1,0:T(8,128)(2,1)} %g_hbm.1), custom_call_target="tpu_custom_call" | custom-call | tf_op jit(solution)/shard_map/window_backward/pallas_call | solution.py:274
  43.1 0.0 copy-start.1
  43.1 0.0 copy-start
  43.1 3.2 %copy.12 = bf16[512,2048]{1,0:T(8,128)(2,1)} copy(bf16[512,2048]{1,0:T(8,128)(2,1)} %get-tuple-element.6) | data formatting | bytes 4194304
  46.4 0.0 copy-done.1
  46.4 0.8 %copy.13 = bf16[512,512]{1,0:T(8,128)(2,1)} copy(bf16[512,512]{1,0:T(8,128)(2,1)S(1)} %copy-done.1) | data formatting | bytes 1048576
  47.2 0.0 copy-done
  47.2 0.8 %copy.14 = bf16[512,512]{1,0:T(8,128)(2,1)} copy(bf16[512,512]{1,0:T(8,128)(2,1)S(1)} %copy-done) | data formatting | bytes 1048576
Async XLA Ops:
  43.1 3.3 %copy-start.1 = (bf16[512,512]{1,0:T(8,128)(2,1)S(1)}, bf16[512,512]{1,0:T(8,128)(2,1)}, u32[]{:S(2)}) copy-start(bf16[512,512]{1,0:T(8,128)(2,1)} %get-tuple-element.7) | copy-start | bytes 1572868
  43.1 4.1 %copy-start = (bf16[512,512]{1,0:T(8,128)(2,1)S(1)}, bf16[512,512]{1,0:T(8,128)(2,1)}, u32[]{:S(2)}) copy-start(bf16[512,512]{1,0:T(8,128)(2,1)} %get-tuple-element.8) | copy-start | bytes 1572868

commit v2 on v1

--- a/solution.py
+++ b/solution.py
@@ -132,9 +132,8 @@
     @pl.when(has_next)
     def _():
         chan_copy.start()
-        for h in range(HK):
-            for copy in forward_copies(h):
-                copy.start()
+        for copy in forward_copies(0):
+            copy.start()
 
     @pl.when(jnp.logical_not(has_prev))
     def _():
@@ -181,47 +180,77 @@
             for copy in forward_copies(h):
                 copy.wait_recv()
 
-        for b in range(blocks):
+        @pl.when(has_next & (h == 0))
+        def _():
+            for ahead in range(1, min(3, HK)):
+                for copy in forward_copies(ahead):
+                    copy.start()
+
+        @pl.when(has_next & (h > 0) & (h < HK - 2))
+        def _():
+            for copy in forward_copies(h + 2):
+                copy.start()
+
+        units = [(b, pair) for b in range(blocks) for pair in range(GROUP // 2)]
+
+        def products(unit):
+            b, pair = unit
             here = slice(b * BLK, (b + 1) * BLK)
             window = slice(b * BLK, b * BLK + span)
+            heads = [h * GROUP + 2 * pair, h * GROUP + 2 * pair + 1]
             key = kw_ref[window, lanes(h, HD)]
             value = vw_ref[window, lanes(h, HD)]
-            bias = bias_ref[b]
-            bias = jnp.concatenate([bias, bias], axis=1)
-            grad_key = None
-            grad_value = None
-            for pair in range(GROUP // 2):
-                heads = [h * GROUP + 2 * pair, h * GROUP + 2 * pair + 1]
-                query = jnp.concatenate([q_ref[here, lanes(i, HD)] for i in heads], axis=0)
-                grad = jnp.concatenate([g_ref[here, lanes(i, HD)] for i in heads], axis=0)
-                scores = (
-                    lax.dot_general(key, query, TRANS_B, preferred_element_type=jnp.float32) + bias
-                )
-                top = jnp.max(scores, axis=0, keepdims=True)
-                weights = jnp.exp2((scores - top) * EXP2_SCALE)
-                probs = weights * (1.0 / jnp.sum(weights, axis=0, keepdims=True))
-                dprobs = lax.dot_general(value, grad, TRANS_B, preferred_element_type=jnp.float32)
-                delta = jnp.sum(probs * dprobs, axis=0, keepdims=True)
-                dscores = (probs * (dprobs - delta)).astype(jnp.bfloat16)
-                probs_low = probs.astype(jnp.bfloat16)
-                grad_query = lax.dot_general(
-                    dscores, key, TRANS_A, preferred_element_type=jnp.float32
-                )
-                grad_query = (grad_query * SCALE).astype(jnp.bfloat16)
-                for k, i in enumerate(heads):
-                    gq_ref[here, lanes(i, HD)] = grad_query[k * BLK : (k + 1) * BLK]
-                key_term = jnp.dot(dscores, query, preferred_element_type=jnp.float32)
-                value_term = jnp.dot(probs_low, grad, preferred_element_type=jnp.float32)
-                grad_key = key_term if grad_key is None else grad_key + key_term
-                grad_value = value_term if grad_value is None else grad_value + value_term
+            query = jnp.concatenate([q_ref[here, lanes(i, HD)] for i in heads], axis=0)
+            grad = jnp.concatenate([g_ref[here, lanes(i, HD)] for i in heads], axis=0)
+            scores = lax.dot_general(key, query, TRANS_B, preferred_element_type=jnp.float32)
+            dprobs = lax.dot_general(value, grad, TRANS_B, preferred_element_type=jnp.float32)
+            return scores, dprobs
+
+        def softmax(unit, scores, dprobs):
+            bias = bias_ref[unit[0]]
+            scores = scores + jnp.concatenate([bias, bias], axis=1)
+            top = jnp.max(scores, axis=0, keepdims=True)
+            weights = jnp.exp2((scores - top) * EXP2_SCALE)
+            probs = weights * (1.0 / jnp.sum(weights, axis=0, keepdims=True))
+            delta = jnp.sum(probs * dprobs, axis=0, keepdims=True)
+            dscores = (probs * (dprobs - delta)).astype(jnp.bfloat16)
+            return dscores, probs.astype(jnp.bfloat16)
+
+        def gradients(unit, dscores, probs_low):
+            b, pair = unit
+            here = slice(b * BLK, (b + 1) * BLK)
+            window = slice(b * BLK, b * BLK + span)
+            heads = [h * GROUP + 2 * pair, h * GROUP + 2 * pair + 1]
+            key = kw_ref[window, lanes(h, HD)]
+            query = jnp.concatenate([q_ref[here, lanes(i, HD)] for i in heads], axis=0)
+            grad = jnp.concatenate([g_ref[here, lanes(i, HD)] for i in heads], axis=0)
+            grad_query = lax.dot_general(key, dscores, TRANS_A, preferred_element_type=jnp.float32)
+            grad_query = jnp.transpose((grad_query * SCALE).astype(jnp.bfloat16))
+            for k, i in enumerate(heads):
+                gq_ref[here, lanes(i, HD)] = grad_query[k * BLK : (k + 1) * BLK]
+            key_term = jnp.dot(dscores, query, preferred_element_type=jnp.float32)
+            value_term = jnp.dot(probs_low, grad, preferred_element_type=jnp.float32)
             shared = slice(b * BLK, b * BLK + rows)
             fresh = slice(b * BLK + rows, b * BLK + span)
-            for total, term in ((dk_ref, grad_key), (dv_ref, grad_value)):
-                if b == 0:
-                    total[h, shared, :] = term[:rows]
+            for total, term in ((dk_ref, key_term), (dv_ref, value_term)):
+                if unit == (0, 0):
+                    total[h, 0:span, :] = term
+                elif pair == 0:
+                    total[h, shared, :] += term[:rows]
+                    total[h, fresh, :] = term[rows:]
                 else:
-                    total[h, shared, :] += term[:rows]
-                total[h, fresh, :] = term[rows:]
+                    total[h, b * BLK : b * BLK + span, :] += term
+
+        ready = products(units[0])
+        done = None
+        for at, unit in enumerate(units):
+            later = products(units[at + 1]) if at + 1 < len(units) else None
+            low = softmax(unit, *ready)
+            if done is not None:
+                gradients(*done)
+            done = (unit, *low)
+            ready = later
+        gradients(*done)
 
         back_send[h, 0] = (dk_ref[h, 0:rows, :] * SCALE).astype(jnp.bfloat16)
         back_send[h, 1] = dv_ref[h, 0:rows, :].astype(jnp.bfloat16)

time: 48.2 us -> 41.7 us (0.87)
  Pallas kernels: 42.5 us -> 36 us
    pallas_call x1, Pallas kernels: 42.5 us -> 36 us  [per_device(): pl.pallas_call(functools.partial(kernel, lax.axis_size('ctx')), out_shape...]
where the time goes in v2:
time: 41.7 us; the launch traced here: 41.5 us
  Pallas kernels  36 us (86%)
  local copies, waits for them, and re-layouts  4.84 us (12%)
  between operations  0.66 us (2%)
    pallas_call x1, Pallas kernels, per_device(): pl.pallas_call(functools.partial(kernel, lax.axis_size('ctx')), out_shape...  36 us
    unnamed x7, local copies, waits for them, and re-layouts  4.84 us

profile of v2, /device:TPU:13, one launch (start us, length us, event | category | flops | bytes accessed | tf_op | source)
XLA Modules:
  0.0 41.5 jit_solution(16057092786698855272)
XLA Ops:
  0.6 36.0 %window_backward.1 = (bf16[512,2048]{1,0:T(8,128)(2,1)}, bf16[512,512]{1,0:T(8,128)(2,1)}, bf16[512,512]{1,0:T(8,128)(2,1)}) custom-call(s32[16]{0:T(128)} %seg_ref.1, s32[1,512]{1,0:T(1,128)} %bitcast.1, bf16[512,2048]{1,0:T(8,128)(2,1)} %q_hbm.1, bf16[512,512]{1,0:T(8,128)(2,1)} %k_hbm.1, bf16[512,512]{1,0:T(8,128)(2,1)} %v_hbm.1, bf16[512,2048]{1,0:T(8,128)(2,1)} %g_hbm.1), custom_call_target="tpu_custom_call" | custom-call | tf_op jit(solution)/shard_map/window_backward/pallas_call | solution.py:303
  36.6 0.0 copy-start.1
  36.6 0.0 copy-start
  36.6 3.2 %copy.12 = bf16[512,2048]{1,0:T(8,128)(2,1)} copy(bf16[512,2048]{1,0:T(8,128)(2,1)} %get-tuple-element.6) | data formatting | bytes 4194304
  39.9 0.0 copy-done.1
  39.9 0.8 %copy.13 = bf16[512,512]{1,0:T(8,128)(2,1)} copy(bf16[512,512]{1,0:T(8,128)(2,1)S(1)} %copy-done.1) | data formatting | bytes 1048576
  40.7 0.0 copy-done
  40.7 0.8 %copy.14 = bf16[512,512]{1,0:T(8,128)(2,1)} copy(bf16[512,512]{1,0:T(8,128)(2,1)S(1)} %copy-done) | data formatting | bytes 1048576
Async XLA Ops:
  36.6 3.3 %copy-start.1 = (bf16[512,512]{1,0:T(8,128)(2,1)S(1)}, bf16[512,512]{1,0:T(8,128)(2,1)}, u32[]{:S(2)}) copy-start(bf16[512,512]{1,0:T(8,128)(2,1)} %get-tuple-element.7) | copy-start | bytes 1572868
  36.6 4.1 %copy-start = (bf16[512,512]{1,0:T(8,128)(2,1)S(1)}, bf16[512,512]{1,0:T(8,128)(2,1)}, u32[]{:S(2)}) copy-start(bf16[512,512]{1,0:T(8,128)(2,1)} %get-tuple-element.8) | copy-start | bytes 1572868

commit v3 on v2

--- a/solution.py
+++ b/solution.py
@@ -294,18 +294,31 @@
             back_copy(h).wait_send()
 
 
+def store(gq_ref, gk_ref, gv_ref, gq_hbm, gk_hbm, gv_hbm, sem):
+    copies = [
+        pltpu.make_async_copy(source, target, sem.at[at])
+        for at, (source, target) in enumerate(
+            ((gq_ref, gq_hbm), (gk_ref, gk_hbm), (gv_ref, gv_hbm))
+        )
+    ]
+    for copy in copies:
+        copy.start()
+    for copy in copies:
+        copy.wait()
+
+
 def per_device(queries, keys, values, grad_out, seg_starts, channels):
     rows = queries.shape[0]
     blocks = rows // BLK
     span = rows + BLK
     vmem = pl.BlockSpec(memory_space=pltpu.VMEM)
     hbm = pl.BlockSpec(memory_space=pl.ANY)
-    return pl.pallas_call(
+    held = pl.pallas_call(
         functools.partial(kernel, lax.axis_size("ctx")),
         out_shape=(
-            jax.ShapeDtypeStruct(queries.shape, jnp.bfloat16),
-            jax.ShapeDtypeStruct(keys.shape, jnp.bfloat16),
-            jax.ShapeDtypeStruct(values.shape, jnp.bfloat16),
+            pltpu.VMEM(queries.shape, jnp.bfloat16),
+            pltpu.VMEM(keys.shape, jnp.bfloat16),
+            pltpu.VMEM(values.shape, jnp.bfloat16),
         ),
         in_specs=[pl.BlockSpec(memory_space=pltpu.SMEM), vmem, hbm, hbm, hbm, hbm],
         out_specs=(vmem, vmem, vmem),
@@ -328,10 +341,19 @@
             pltpu.SemaphoreType.DMA((HK,)),
         ],
         compiler_params=pltpu.CompilerParams(
-            collective_id=0, has_side_effects=True, vmem_limit_bytes=56 * 1024 * 1024
+            collective_id=0, has_side_effects=True, vmem_limit_bytes=60 * 1024 * 1024
         ),
         name="window_backward",
     )(seg_starts, channels.reshape(1, rows), queries, keys, values, grad_out)
+    return pl.pallas_call(
+        store,
+        out_shape=tuple(jax.ShapeDtypeStruct(x.shape, x.dtype) for x in (queries, keys, values)),
+        in_specs=[pl.BlockSpec(memory_space=pl.ANY)] * 3,
+        out_specs=(hbm,) * 3,
+        scratch_shapes=[pltpu.SemaphoreType.DMA((3,))],
+        compiler_params=pltpu.CompilerParams(vmem_limit_bytes=2 * 1024 * 1024),
+        name="store",
+    )(*held)
 
 
 def solution(mesh):

time: 41.7 us -> 36.8 us (0.88)
  local copies, waits for them, and re-layouts: 4.84 us -> 0 us
    unnamed x7 -> x0, local copies, waits for them, and re-layouts: 4.84 us -> none
    pallas_call x0 -> x1, Pallas kernels: none -> 1.68 us  [per_device(): pl.pallas_call(store, out_shape=tuple((jax.ShapeDtypeStruct(x.shape, x.dt...]
    pallas_call x1, Pallas kernels: 36 us -> 34.3 us  [per_device(): pl.pallas_call(functools.partial(kernel, lax.axis_size('ctx')), out_shape...]
where the time goes in v3:
time: 36.8 us; the launch traced here: 36.7 us
  Pallas kernels  36 us (98%)
  between operations  0.64 us (2%)
    pallas_call x1, Pallas kernels, per_device(): pl.pallas_call(functools.partial(kernel, lax.axis_size('ctx')), out_shape...  34.3 us
    pallas_call x1, Pallas kernels, per_device(): pl.pallas_call(store, out_shape=tuple((jax.ShapeDtypeStruct(x.shape, x.dt...  1.68 us

profile of v3, /device:TPU:13, one launch (start us, length us, event | category | flops | bytes accessed | tf_op | source)
XLA Modules:
  0.0 36.7 jit_solution(9644408253759086266)
XLA Ops:
  0.6 34.3 %window_backward.1 = (bf16[512,2048]{1,0:T(8,128)(2,1)S(1)}, bf16[512,512]{1,0:T(8,128)(2,1)S(1)}, bf16[512,512]{1,0:T(8,128)(2,1)S(1)}) custom-call(s32[16]{0:T(128)} %seg_ref.1, s32[1,512]{1,0:T(1,128)} %bitcast.1, bf16[512,2048]{1,0:T(8,128)(2,1)} %q_hbm.1, bf16[512,512]{1,0:T(8,128)(2,1)} %k_hbm.1, bf16[512,512]{1,0:T(8,128)(2,1)} %v_hbm.1, ...), custom_call_target="tpu_custom_call" | custom-call | tf_op jit(solution)/shard_map/window_backward/pallas_call | solution.py:316
  35.0 1.7 %store.1 = (bf16[512,2048]{1,0:T(8,128)(2,1)}, bf16[512,512]{1,0:T(8,128)(2,1)}, bf16[512,512]{1,0:T(8,128)(2,1)}) custom-call(bf16[512,2048]{1,0:T(8,128)(2,1)S(1)} %get-tuple-element.6.gq_ref, bf16[512,512]{1,0:T(8,128)(2,1)S(1)} %get-tuple-element.7.gk_ref, bf16[512,512]{1,0:T(8,128)(2,1)S(1)} %get-tuple-element.8.gv_ref), custom_call_target="tpu_custom_call" | custom-call | tf_op jit(solution)/shard_map/store/pallas_call | solution.py:348

commit v4 on v3

--- a/solution.py
+++ b/solution.py
@@ -211,8 +211,9 @@
             scores = scores + jnp.concatenate([bias, bias], axis=1)
             top = jnp.max(scores, axis=0, keepdims=True)
             weights = jnp.exp2((scores - top) * EXP2_SCALE)
-            probs = weights * (1.0 / jnp.sum(weights, axis=0, keepdims=True))
-            delta = jnp.sum(probs * dprobs, axis=0, keepdims=True)
+            inverse = 1.0 / jnp.sum(weights, axis=0, keepdims=True)
+            delta = jnp.sum(weights * dprobs, axis=0, keepdims=True) * inverse
+            probs = weights * inverse
             dscores = (probs * (dprobs - delta)).astype(jnp.bfloat16)
             return dscores, probs.astype(jnp.bfloat16)
 

time: 36.8 us -> 36.7 us (level)
  no operation moved by 1% of the time
where the time goes in v4:
time: 36.7 us; the launch traced here: 36.6 us
  Pallas kernels  35.9 us (98%)
  between operations  0.64 us (2%)
    pallas_call x1, Pallas kernels, per_device(): pl.pallas_call(functools.partial(kernel, lax.axis_size('ctx')), out_shape...  34.2 us
    pallas_call x1, Pallas kernels, per_device(): pl.pallas_call(store, out_shape=tuple((jax.ShapeDtypeStruct(x.shape, x.dt...  1.68 us

profile of v4, /device:TPU:13, one launch (start us, length us, event | category | flops | bytes accessed | tf_op | source)
XLA Modules:
  0.0 36.6 jit_solution(3638544179857362726)
XLA Ops:
  0.6 34.2 %window_backward.1 = (bf16[512,2048]{1,0:T(8,128)(2,1)S(1)}, bf16[512,512]{1,0:T(8,128)(2,1)S(1)}, bf16[512,512]{1,0:T(8,128)(2,1)S(1)}) custom-call(s32[16]{0:T(128)} %seg_ref.1, s32[1,512]{1,0:T(1,128)} %bitcast.1, bf16[512,2048]{1,0:T(8,128)(2,1)} %q_hbm.1, bf16[512,512]{1,0:T(8,128)(2,1)} %k_hbm.1, bf16[512,512]{1,0:T(8,128)(2,1)} %v_hbm.1, ...), custom_call_target="tpu_custom_call" | custom-call | tf_op jit(solution)/shard_map/window_backward/pallas_call | solution.py:317
  34.9 1.7 %store.1 = (bf16[512,2048]{1,0:T(8,128)(2,1)}, bf16[512,512]{1,0:T(8,128)(2,1)}, bf16[512,512]{1,0:T(8,128)(2,1)}) custom-call(bf16[512,2048]{1,0:T(8,128)(2,1)S(1)} %get-tuple-element.6.gq_ref, bf16[512,512]{1,0:T(8,128)(2,1)S(1)} %get-tuple-element.7.gk_ref, bf16[512,512]{1,0:T(8,128)(2,1)S(1)} %get-tuple-element.8.gv_ref), custom_call_target="tpu_custom_call" | custom-call | tf_op jit(solution)/shard_map/store/pallas_call | solution.py:349
